TPU v7x, 32 devices: a whole 2x2x4 slice. The times are simulated.
32 devices in a mesh: groups: 2 (over y), tm: 4 (over z), head: 2 (over x), mp: 2 (over core).
Axes of the slice: x: 2, y: 2, z: 4, core: 2. Of those that a mesh axis runs over, the one named last changes fastest.
Arguments:
- queries: bfloat16 [2048, 2048], P(('groups', 'tm'), ('head', 'mp')), parts along dimension 0, may hold values from -6 to 6
- key_rows: bfloat16 [2048, 2048], P(('groups', 'tm'), ('head', 'mp')), parts along dimension 0, may hold values from -6 to 6
- value_rows: bfloat16 [2048, 2048], P(('groups', 'tm'), ('head', 'mp')), parts along dimension 0, may hold values from -12 to 12
- cotangent: bfloat16 [2048, 2048], P(('groups', 'tm'), ('head', 'mp')), parts along dimension 0, may hold values from -12 to 12
- block_active: int32 [16], P('groups'), parts along dimension 0, may hold values from 0 to 1
- send_counts: int32 [8, 2], P('groups'), parts along dimension 0, may hold values from 0 to 1, as said below
- block_mask: int32 [16, 8], P('groups'), parts along dimension 0, may hold values from 0 to 1, as said below
Outputs:
- attended: bfloat16 [4096, 2048], P(('groups', 'tm'), ('head', 'mp')), parts along dimension 0
- query_grad: bfloat16 [4096, 2048], P(('groups', 'tm'), ('head', 'mp')), parts along dimension 0
- key_grad: bfloat16 [2048, 2048], P(('groups', 'tm'), ('head', 'mp')), parts along dimension 0
- value_grad: bfloat16 [2048, 2048], P(('groups', 'tm'), ('head', 'mp')), parts along dimension 0
There are 2 independent parts, one for each index of `groups`. A program takes and returns all parts, laid end to end along the dimension named above; each array names one. Nothing has to cross between parts.
Inputs may be any that keep to these rules, and one draw needn't show every extreme that they name: `send_counts`: column 0 of row i counts the first blocks of shard i that go to shard i-1, column 1 its last blocks that go to shard i+1 (shard 0 follows shard 4-1); the two sum to at most 2; every block that is handed on is active. `block_mask`: the diagonal is 1.
All inputs are finite; a program needn't handle non-finite values.
Results may differ from a plain program's by a relative error of at most 0.02.
Values may be sent and summed in bfloat16 or wider, within the bound.
A program may use at most 64 MiB of HBM per device.

v0:
```python
import math
import jax
import jax.numpy as jnp
from jax import lax
from jax.sharding import PartitionSpec as P

HD = 128
BLK = 128
CAP = 1
very_low = -1e30


def extended_2(shard, sides, width):
    for axis, dim in sides:
        peers, length = (lax.axis_size(axis), shard.shape[dim])
        up = [(i, (i + 1) % peers) for i in range(peers)]
        down = [(j, i) for i, j in up]
        last = lax.slice_in_dim(shard, length - width, length, axis=dim)
        first = lax.slice_in_dim(shard, 0, width, axis=dim)
        before = lax.ppermute(last, axis, up)
        after = lax.ppermute(first, axis, down)
        shard = jnp.concatenate([before, shard, after], axis=dim)
    return shard


def pick(table, positions, extent):
    matches = positions[:, None] == jnp.arange(extent, dtype=jnp.int32)[None, :]
    return jnp.sum(jnp.where(matches, table[None, :], 0), axis=1)


def slot_layout(block_active, send_counts, block_mask, shards, own_blocks, capacity):
    slot_count = own_blocks + 2 * capacity
    all_blocks = shards * own_blocks
    places = jnp.arange(shards * slot_count, dtype=jnp.int32)
    device = places // slot_count
    slot_index = places % slot_count
    before = (device + shards - 1) % shards
    following = (device + 1) % shards
    to_left = send_counts[:, 0]
    to_right = send_counts[:, 1]
    from_before = slot_index < capacity
    from_after = slot_index >= capacity + own_blocks
    owner_shard = jnp.where(from_before, before, jnp.where(from_after, following, device))
    local_block = jnp.where(
        from_before,
        own_blocks - capacity + slot_index,
        jnp.where(from_after, slot_index - capacity - own_blocks, slot_index - capacity),
    )
    middle_ok = (local_block >= pick(to_left, device, shards)) & (
        local_block < own_blocks - pick(to_right, device, shards)
    )
    holds_record = jnp.where(
        from_before,
        slot_index >= capacity - pick(to_right, before, shards),
        jnp.where(from_after, local_block < pick(to_left, following, shards), middle_ok),
    )
    anchor = owner_shard * own_blocks + local_block
    onehot = (anchor[:, None] == jnp.arange(all_blocks, dtype=jnp.int32)[None, :]).astype(
        jnp.float32
    )
    seeing = (block_mask * block_active[None, :]).astype(jnp.float32)
    block_rows = jnp.dot(onehot, seeing, precision=lax.Precision.HIGHEST)
    active = jnp.dot(onehot, block_active.astype(jnp.float32), precision=lax.Precision.HIGHEST)
    present = jnp.where(holds_record, active, 0.0)
    return (anchor, block_rows * present[:, None], present)


def block_hot(offset, length, extent):
    blocks = (offset + jnp.arange(length, dtype=jnp.int32)) // BLK
    return (blocks[:, None] == jnp.arange(extent, dtype=jnp.int32)[None, :]).astype(jnp.bfloat16)


def sweep(update, running, pieces, offset):
    row_count = pieces[0].shape[0]
    step_rows = math.gcd(row_count, 1024)
    if step_rows == row_count:
        return update(running, pieces, offset)

    def one_turn(turn_index, carried):
        part_pieces = tuple(
            (
                lax.dynamic_slice_in_dim(member, turn_index * step_rows, step_rows, 0)
                for member in pieces
            )
        )
        return update(carried, part_pieces, offset + turn_index * step_rows)

    return lax.fori_loop(0, row_count // step_rows, one_turn, running)


def body(queries, key_rows, value_rows, cotangent, block_active, send_counts, block_mask):
    shards = lax.axis_size("tm")
    shard_index = lax.axis_index("tm")
    model_width = queries.shape[1]
    head_count = model_width // HD
    own_rows = queries.shape[0]
    own_blocks = own_rows // BLK
    all_blocks = block_active.shape[0]
    slot_count = own_blocks + 2 * CAP
    slot_rows = slot_count * BLK
    scaling = 1.0 / math.sqrt(HD)
    anchor, table, present = slot_layout(
        block_active, send_counts, block_mask, shards, own_blocks, CAP
    )
    records = jnp.concatenate([queries, cotangent], axis=1)
    extended = extended_2(records, (("tm", 0),), CAP * BLK)
    query_slots = extended[:, :model_width].reshape(slot_rows, head_count, HD)
    cotan_slots = extended[:, model_width:].reshape(slot_rows, head_count, HD)
    my_table = lax.dynamic_slice_in_dim(table, shard_index * slot_count, slot_count, 0)
    query_table = jnp.repeat(my_table, BLK, axis=0).astype(jnp.bfloat16)
    live = (
        jnp.repeat(lax.dynamic_slice_in_dim(present, shard_index * slot_count, slot_count, 0), BLK)
        > 0.5
    )
    keys_all, values_all = (
        lax.all_gather(key_rows, "tm", axis=0, tiled=True),
        lax.all_gather(value_rows, "tm", axis=0, tiled=True),
    )

    def own_scores(key_piece, offset):
        allowed = (
            lax.dot_general(
                query_table,
                block_hot(offset, key_piece.shape[0], all_blocks),
                (((1,), (1,)), ((), ())),
                preferred_element_type=jnp.float32,
            )[:, None, :]
            > 0.5
        )
        scores = (
            jnp.einsum("qhd,khd->qhk", query_slots, key_piece, preferred_element_type=jnp.float32)
            * scaling
        )
        return (allowed, scores)

    def forward(running, pieces, offset):
        peak, masses, accum = running
        key_piece = pieces[0].reshape(-1, head_count, HD)
        value_piece = pieces[1].reshape(-1, head_count, HD)
        allowed, scores = own_scores(key_piece, offset)
        new_peak = jnp.maximum(peak, jnp.max(jnp.where(allowed, scores, very_low), axis=2))
        weights = jnp.where(
            allowed, jnp.exp(jnp.where(allowed, scores - new_peak[:, :, None], 0.0)), 0.0
        )
        shrink = jnp.exp(peak - new_peak)
        masses = masses * shrink + jnp.sum(weights, axis=2)
        accum = accum * shrink[:, :, None] + jnp.einsum(
            "qhk,khd->qhd",
            weights.astype(jnp.bfloat16),
            value_piece,
            preferred_element_type=jnp.float32,
        )
        return (new_peak, masses, accum)

    initial = (
        jnp.full((slot_rows, head_count), very_low, jnp.float32),
        jnp.zeros((slot_rows, head_count), jnp.float32),
        jnp.zeros((slot_rows, head_count, HD), jnp.float32),
    )
    peak, masses, accum = sweep(forward, initial, (keys_all, values_all), 0)
    denominator = jnp.where(live[:, None], masses, 1.0)
    attended = (accum / denominator[:, :, None]).astype(jnp.bfloat16)
    log_norm = peak + jnp.log(denominator)
    deltas = jnp.sum(cotan_slots.astype(jnp.float32) * attended.astype(jnp.float32), axis=2)

    def own_gradients(key_piece, value_piece, offset):
        allowed, scores = own_scores(key_piece, offset)
        probs = jnp.where(
            allowed, jnp.exp(jnp.where(allowed, scores - log_norm[:, :, None], 0.0)), 0.0
        )
        weight_grad = jnp.einsum(
            "qhd,khd->qhk", cotan_slots, value_piece, preferred_element_type=jnp.float32
        )
        return (probs, (probs * (weight_grad - deltas[:, :, None])).astype(jnp.bfloat16))

    zero_query = jnp.zeros((slot_rows, head_count, HD), jnp.float32)

    def query_pass(query_sum, pieces, offset):
        key_piece = pieces[0].reshape(-1, head_count, HD)
        value_piece = pieces[1].reshape(-1, head_count, HD)
        probs, score_grad = own_gradients(key_piece, value_piece, offset)
        return query_sum + jnp.einsum(
            "qhk,khd->qhd", score_grad, key_piece, preferred_element_type=jnp.float32
        )

    query_sum = sweep(query_pass, zero_query, (keys_all, values_all), 0)
    own_keys = key_rows.reshape(own_rows, head_count, HD)
    own_values = value_rows.reshape(own_rows, head_count, HD)
    own_hot = block_hot(shard_index * own_rows, own_rows, all_blocks)
    slot_table = table.astype(jnp.bfloat16)
    logsum_all, delta_all = (
        lax.all_gather(log_norm, "tm", axis=0, tiled=True),
        lax.all_gather(deltas, "tm", axis=0, tiled=True),
    )

    def owner_work(running, pieces, offset):
        key_sum, value_sum = running
        query_piece, cotan_piece = pieces
        row_count = query_piece.shape[0]
        logsum_piece = lax.dynamic_slice_in_dim(logsum_all, offset, row_count, 0)
        delta_piece = lax.dynamic_slice_in_dim(delta_all, offset, row_count, 0)
        piece_table = jnp.dot(
            block_hot(offset, row_count, shards * slot_count),
            slot_table,
            preferred_element_type=jnp.float32,
        ).astype(jnp.bfloat16)
        allowed = (
            lax.dot_general(
                piece_table, own_hot, (((1,), (1,)), ((), ())), preferred_element_type=jnp.float32
            )[:, None, :]
            > 0.5
        )
        query_three = query_piece.reshape(row_count, head_count, HD)
        cotan_three = cotan_piece.reshape(row_count, head_count, HD)
        scores = (
            jnp.einsum("qhd,khd->qhk", query_three, own_keys, preferred_element_type=jnp.float32)
            * scaling
        )
        probs = jnp.where(
            allowed, jnp.exp(jnp.where(allowed, scores - logsum_piece[:, :, None], 0.0)), 0.0
        )
        weight_grad = jnp.einsum(
            "qhd,khd->qhk", cotan_three, own_values, preferred_element_type=jnp.float32
        )
        score_grad = (probs * (weight_grad - delta_piece[:, :, None])).astype(jnp.bfloat16)
        key_sum = key_sum + jnp.einsum(
            "qhk,qhd->khd", score_grad, query_three, preferred_element_type=jnp.float32
        )
        value_sum = value_sum + jnp.einsum(
            "qhk,qhd->khd",
            probs.astype(jnp.bfloat16),
            cotan_three,
            preferred_element_type=jnp.float32,
        )
        return (key_sum, value_sum)

    key_zero = jnp.zeros((own_rows, head_count, HD), jnp.float32)
    key_sum, value_sum = sweep(
        owner_work,
        (key_zero, key_zero),
        (
            lax.all_gather(query_slots.reshape(slot_rows, model_width), "tm", axis=0, tiled=True),
            lax.all_gather(cotan_slots.reshape(slot_rows, model_width), "tm", axis=0, tiled=True),
        ),
        jnp.int32(0),
    )
    key_grad = (key_sum * scaling).astype(jnp.bfloat16).reshape(own_rows, model_width)
    value_grad = value_sum.astype(jnp.bfloat16).reshape(own_rows, model_width)
    query_grad = (query_sum * scaling).astype(jnp.bfloat16).reshape(slot_rows, model_width)
    return (attended.reshape(slot_rows, model_width), query_grad, key_grad, value_grad)


def solution(mesh):
    in_specs = (
        P(("groups", "tm"), ("head", "mp")),
        P(("groups", "tm"), ("head", "mp")),
        P(("groups", "tm"), ("head", "mp")),
        P(("groups", "tm"), ("head", "mp")),
        P("groups"),
        P("groups", None),
        P("groups", None),
    )
    out_specs = (
        P(("groups", "tm"), ("head", "mp")),
        P(("groups", "tm"), ("head", "mp")),
        P(("groups", "tm"), ("head", "mp")),
        P(("groups", "tm"), ("head", "mp")),
    )
    return jax.shard_map(body, mesh=mesh, in_specs=in_specs, out_specs=out_specs, check_vma=False)
```

profile of v0, /device:TPU:0, one launch (start us, length us, event | category | flops | bytes accessed | tf_op | source)
XLA Modules:
  0.0 210.3 jit_solution(11697124278992950127)
XLA Ops:
  7.2 0.0 copy-start.5
  7.2 0.0 copy-start.10
  7.2 0.0 copy-start.12
  7.2 0.0 copy-start.11
  7.2 0.0 all-gather.5.cloned.1.call-start
  7.3 1.8 copy.78
  9.1 0.0 all-gather.5.cloned.1.call-update
  9.1 0.0 all-gather.7.cloned.1.call-start
  9.2 0.7 all-gather.7.cloned.1.call-update
  9.9 0.0 all-gather.9.cloned.1.call-start
  9.9 1.1 copy.76
  11.0 1.1 copy.77
  12.1 5.1 %collective-permute-start.1 = (bf16[128,1024]{0,1:T(8,128)(2,1)S(1)}, bf16[128,1024]{0,1:T(8,128)(2,1)S(1)}, u32[]{:S(2)}, u32[]{:S(2)}) collective-permute-start(bf16[128,1024]{0,1:T(8,128)(2,1)S(1)} %get-tuple-element.421), channel_id=1, source_target_pairs={{4,0},{8,4},{12,8},{0,12},{5,1},{9,5},{13,9},{1,13},{6,2},{10,6},{... | collective-permute-start | bytes 786440 | tf_op jit(solution)/shard_map/ppermute | solution.py:21
  17.2 0.0 collective-permute-start
  17.2 9.6 %collective-permute-done.1 = bf16[128,1024]{0,1:T(8,128)(2,1)S(1)} collective-permute-done((bf16[128,1024]{0,1:T(8,128)(2,1)S(1)}, bf16[128,1024]{0,1:T(8,128)(2,1)S(1)}, u32[]{:S(2)}, u32[]{:S(2)}) %collective-permute-start.1) | collective-permute-done | bytes 262176 | tf_op jit(solution)/shard_map/ppermute | solution.py:21
  26.8 10.1 %collective-permute-done = bf16[128,1024]{0,1:T(8,128)(2,1)S(1)} collective-permute-done((bf16[128,1024]{0,1:T(8,128)(2,1)S(1)}, bf16[128,1024]{0,1:T(8,128)(2,1)S(1)}, u32[]{:S(2)}, u32[]{:S(2)}) %collective-permute-start) | collective-permute-done | bytes 262176 | tf_op jit(solution)/shard_map/ppermute | solution.py:20
  37.0 0.1 pad_maximum_fusion
  37.1 1.1 fusion.82
  38.2 0.0 all-gather.9.cloned.1.call-update
  38.2 0.0 all-gather.11.cloned.1.call-start
  38.3 0.1 copy.85
  38.5 0.1 select_reduce_fusion.3
  38.6 0.2 fusion.63
  38.7 0.0 copy-done.11
  38.8 0.2 convolution_multiply_fusion
  38.9 0.1 copy.86
  39.0 0.2 copy.87
  39.2 0.8 copy.88
  40.1 0.1 dynamic-slice_compare_fusion
  40.2 0.1 broadcast_bitcast_fusion
  40.3 0.6 convolution_compare_fusion.1
  40.8 0.0 all-gather.11.cloned.1.call-update
  40.9 7.4 %all-gather.5.cloned.1.call-done = bf16[1024,512]{0,1:T(8,128)(2,1)} async-done(((bf16[256,512]{0,1:T(8,128)(2,1)}), bf16[1024,512]{0,1:T(8,128)(2,1)}) %all-gather.5.cloned.1.call-update) | async-done | bytes 1048592 | tf_op jit(solution)/shard_map/all_gather | solution.py:116
  48.3 0.0 copy-done.1
  48.3 6.2 %fusion.34 = (f32[512,4]{0,1:T(4,128)S(1)}, f32[4,512,1024]{2,1,0:T(8,128)}) fusion(pred[512,1024]{1,0:T(8,128)(4,1)S(1)} %convolution_compare_fusion.1, bf16[512,4,128]{0,2,1:T(8,128)(2,1)S(1)} %bitcast.173, bf16[1024,4,128]{0,2,1:T(8,128)(2,1)} %bitcast.176), kind=kOutput, calls=%fused_computation.46 | convolution fusion | flops 543160320 | bytes 10493952 | tf_op jit(solution)/shard_map/qhd,khd->qhk/dot_general | solution.py:131
  54.5 22.5 %all-gather.7.cloned.1.call-done = bf16[1024,512]{1,0:T(8,128)(2,1)} async-done(((bf16[256,512]{1,0:T(8,128)(2,1)}), bf16[1024,512]{1,0:T(8,128)(2,1)}) %all-gather.7.cloned.1.call-update) | async-done | bytes 1048592 | tf_op jit(solution)/shard_map/all_gather | solution.py:117
  77.1 2.3 %copy.81 = bf16[1024,512]{0,1:T(8,128)(2,1)} copy(bf16[1024,512]{1,0:T(8,128)(2,1)} %all-gather.7.cloned.1.call-done) | data formatting | bytes 2097152 | tf_op jit(solution)/shard_map/all_gather | solution.py:117
  79.4 5.3 %fusion.41 = f32[512,4]{0,1:T(4,128)S(1)} fusion(f32[4,512,1024]{2,1,0:T(8,128)} %get-tuple-element.426, f32[512,4]{0,1:T(4,128)S(1)} %broadcast_maximum_fusion, pred[512,1024]{1,0:T(8,128)(4,1)S(1)} %convolution_compare_fusion.1), kind=kLoop, calls=%fused_computation.53 | loop fusion | flops 10483712 | bytes 8929280 | tf_op jit(solution)/shard_map/reduce_sum | solution.py:146
  84.7 0.6 copy-done
  85.3 5.0 %multiply_reduce_fusion = (f32[512,4]{0,1:T(4,128)S(1)}, bf16[512,4,128]{0,2,1:T(8,128)(2,1)}) fusion(bf16[512,1024]{0,1:T(8,128)(2,1)S(1)} %pad_maximum_fusion, f32[512,4]{0,1:T(4,128)S(1)} %get-tuple-element.413, bf16[1024,4,128]{0,2,1:T(8,128)(2,1)} %bitcast.180, f32[4,512,1024]{2,1,0:T(8,128)S(1)} %copy-done, f32[512,4]{0,1:T(4,128)S(1)} %broadcast_maximum_fusion, ...), kind=kOutput, calls=%fused_computation.69 | convolution fusion | flops 549189632 | bytes 11042816 | tf_op jit(solution)/shard_map/qhk,khd->qhd/dot_general | solution.py:147
  90.3 2.0 copy.91
  92.4 0.0 copy-done.4
  92.4 8.0 %fusion.60 = bf16[4,512,128]{1,2,0:T(8,128)(2,1)S(1)} fusion(bf16[1024,4,128]{0,2,1:T(8,128)(2,1)S(1)} %bitcast.177, f32[4,512,1024]{2,1,0:T(8,128)} %get-tuple-element.426, f32[512,4]{0,1:T(4,128)S(1)} %get-tuple-element.427, f32[512,4]{0,1:T(4,128)S(1)} %get-tuple-element.412, pred[512,1024]{1,0:T(8,128)(4,1)S(1)} %convolution_compare_fusion.1, ...), kind=kOutput, calls=%fused_computation.64 | convolution fusion | flops 1088946176 | bytes 12075008 | tf_op jit(solution)/shard_map/qhk,khd->qhd/dot_general | solution.py:182
  100.4 1.0 copy.92
  101.4 13.4 %all_gather.21 = f32[2048,4]{0,1:T(4,128)S(1)} all-gather(f32[512,4]{0,1:T(4,128)S(1)} %get-tuple-element.412), channel_id=1, replica_groups=mesh['groups'=2,'tm'=4,'head'=2,'mp'=2] {'tm'}, dimensions={0}, use_global_device_ids=true | all-gather | bytes 40960 | tf_op jit(solution)/shard_map/all_gather | solution.py:192
  114.7 13.3 %all_gather.23 = f32[2048,4]{0,1:T(4,128)S(1)} all-gather(f32[512,4]{0,1:T(4,128)S(1)} %get-tuple-element.427), channel_id=1, replica_groups=mesh['groups'=2,'tm'=4,'head'=2,'mp'=2] {'tm'}, dimensions={0}, use_global_device_ids=true | all-gather | bytes 40960 | tf_op jit(solution)/shard_map/all_gather | solution.py:193
  128.0 43.1 %all-gather.11.cloned.1.call-done = bf16[2048,512]{0,1:T(8,128)(2,1)} async-done(((bf16[512,512]{0,1:T(8,128)(2,1)}), bf16[2048,512]{0,1:T(8,128)(2,1)}) %all-gather.11.cloned.1.call-update) | async-done | bytes 2097168 | tf_op jit(solution)/shard_map/all_gather | solution.py:243
  171.1 28.8 %while.18 = (s32[]{:T(128)}, f32[256,4,128]{0,2,1:T(8,128)}, f32[256,4,128]{0,2,1:T(8,128)}, bf16[2048,512]{0,1:T(8,128)(2,1)}, bf16[16,8]{0,1:T(8,128)(2,1)S(1)...) while((s32[]{:T(128)}, f32[256,4,128]{0,2,1:T(8,128)}, ...), condition=%wide.region_8.9_spmd.clone, body=%wide.region_7.8_spmd.clone.sunk | while | flops 1091612672 | bytes 32892488 | solution.py:88
  171.1 1.7 constant_dynamic-slice_fusion.6
  172.9 2.7 %fusion.119 = f32[4,1024,256]{2,1,0:T(8,128)} fusion(bf16[1024,4,128]{0,2,1:T(8,128)(2,1)S(1)} %bitcast.169, bf16[256,4,128]{2,0,1:T(8,128)(2,1)S(1)} %get-tuple-element.541), kind=kOutput, calls=%fused_computation.134.clone.1 | convolution fusion | flops 268435456 | bytes 5505024 | tf_op jit(solution)/shard_map/while/body/eval_jaxpr/qhd,khd->qhk/dot_general | solution.py:216
  175.6 1.3 convolution_compare_fusion.3
  176.9 4.5 %fusion.120 = f32[256,4,128]{0,2,1:T(8,128)S(1)} fusion(bf16[1024,4,128]{0,2,1:T(8,128)(2,1)S(1)} %bitcast.170, f32[4,1024,256]{2,1,0:T(8,128)} %fusion.119, bf16[1024,4,128]{0,2,1:T(8,128)(2,1)S(1)} %bitcast.171, bf16[256,4,128]{2,0,1:T(8,128)(2,1)} %get-tuple-element.544, f32[1024,4]{0,1:T(4,128)S(1)} %get-tuple-element.504, ...), kind=kOutput, calls=%fused_computation.16.clone.1 | convolution fusion | flops 544473088 | bytes 7897089 | tf_op jit(solution)/shard_map/while/body/eval_jaxpr/qhk,qhd->khd/dot_general | solution.py:226
  181.5 3.2 %fusion.121 = f32[256,4,128]{0,2,1:T(8,128)S(1)} fusion(bf16[1024,4,128]{0,2,1:T(8,128)(2,1)S(1)} %bitcast.172, f32[4,1024,256]{2,1,0:T(8,128)} %fusion.119, f32[1024,4]{0,1:T(4,128)S(1)} %get-tuple-element.505, pred[1024,256]{1,0:T(8,128)(4,1)} %convolution_compare_fusion.3, f32[256,4,128]{0,2,1:T(8,128)S(1)} %copy-done.8, pred[]{:T(512)S(6)} %compare.53), kind=kOutput, calls=%fused_computation.15.clone.1 | convolution fusion | flops 273940480 | bytes 6569985 | tf_op jit(solution)/shard_map/while/body/eval_jaxpr/qhk,qhd->khd/dot_general | solution.py:229
  184.7 0.8 copy-done.9
  185.5 1.7 constant_dynamic-slice_fusion.6
  187.3 2.7 %fusion.119 = f32[4,1024,256]{2,1,0:T(8,128)} fusion(bf16[1024,4,128]{0,2,1:T(8,128)(2,1)S(1)} %bitcast.169, bf16[256,4,128]{2,0,1:T(8,128)(2,1)S(1)} %get-tuple-element.541), kind=kOutput, calls=%fused_computation.134.clone.1 | convolution fusion | flops 268435456 | bytes 5505024 | tf_op jit(solution)/shard_map/while/body/eval_jaxpr/qhd,khd->qhk/dot_general | solution.py:216
  190.0 1.3 convolution_compare_fusion.3
  191.3 4.5 %fusion.120 = f32[256,4,128]{0,2,1:T(8,128)S(1)} fusion(bf16[1024,4,128]{0,2,1:T(8,128)(2,1)S(1)} %bitcast.170, f32[4,1024,256]{2,1,0:T(8,128)} %fusion.119, bf16[1024,4,128]{0,2,1:T(8,128)(2,1)S(1)} %bitcast.171, bf16[256,4,128]{2,0,1:T(8,128)(2,1)} %get-tuple-element.544, f32[1024,4]{0,1:T(4,128)S(1)} %get-tuple-element.504, ...), kind=kOutput, calls=%fused_computation.16.clone.1 | convolution fusion | flops 544473088 | bytes 7897089 | tf_op jit(solution)/shard_map/while/body/eval_jaxpr/qhk,qhd->khd/dot_general | solution.py:226
  195.9 3.2 %fusion.121 = f32[256,4,128]{0,2,1:T(8,128)S(1)} fusion(bf16[1024,4,128]{0,2,1:T(8,128)(2,1)S(1)} %bitcast.172, f32[4,1024,256]{2,1,0:T(8,128)} %fusion.119, f32[1024,4]{0,1:T(4,128)S(1)} %get-tuple-element.505, pred[1024,256]{1,0:T(8,128)(4,1)} %convolution_compare_fusion.3, f32[256,4,128]{0,2,1:T(8,128)S(1)} %copy-done.8, pred[]{:T(512)S(6)} %compare.53), kind=kOutput, calls=%fused_computation.15.clone.1 | convolution fusion | flops 273940480 | bytes 6569985 | tf_op jit(solution)/shard_map/while/body/eval_jaxpr/qhk,qhd->khd/dot_general | solution.py:229
  199.1 0.8 copy-done.9
  199.9 1.1 multiply_convert_fusion
  201.0 0.8 copy.100
  201.9 1.1 convert_element_type.96
  202.9 0.8 copy.101
  (42 shorter events, 0.2 us)
Async XLA Ops:
  7.2 31.1 %copy-start.5 = (bf16[256,512]{1,0:T(8,128)(2,1)S(1)}, bf16[256,512]{1,0:T(8,128)(2,1)}, u32[]{:S(2)}) copy-start(bf16[256,512]{1,0:T(8,128)(2,1)} %param.11) | copy-start | bytes 786436
  7.2 31.3 %copy-start.10 = (s32[4,2]{0,1:T(2,128)S(1)}, s32[4,2]{0,1:T(2,128)}, u32[]{:S(2)}) copy-start(s32[4,2]{0,1:T(2,128)} %param.14) | copy-start | bytes 100
  7.2 31.4 %copy-start.12 = (s32[8]{0:T(128)S(1)}, s32[8]{0:T(128)}, u32[]{:S(2)}) copy-start(s32[8]{0:T(128)} %param.13) | copy-start | bytes 100
  7.2 31.6 %copy-start.11 = (s32[8,8]{1,0:T(8,128)S(1)}, s32[8,8]{1,0:T(8,128)}, u32[]{:S(2)}) copy-start(s32[8,8]{1,0:T(8,128)} %param.15) | copy-start | bytes 772
  7.2 41.1 %all-gather.5.cloned.1.call-start = ((), (), s32[]{:S(2)}) async-start(), calls=%async_computation | async-start | bytes 1310720 | tf_op jit(solution)/shard_map/all_gather | solution.py:116
  9.1 30.0 %copy-start.2 = (bf16[256,512]{0,1:T(8,128)(2,1)S(1)}, bf16[256,512]{0,1:T(8,128)(2,1)}, u32[]{:S(2)}) copy-start(bf16[256,512]{0,1:T(8,128)(2,1)} %copy.78) | copy-start | bytes 786436
  9.1 67.9 %all-gather.7.cloned.1.call-start = ((), (), s32[]{:S(2)}) async-start(), calls=%async_computation.1 | async-start | bytes 1310720 | tf_op jit(solution)/shard_map/all_gather | solution.py:117
  9.9 118.2 %all-gather.9.cloned.1.call-start = ((), (), s32[]{:S(2)}) async-start(), calls=%async_computation.2 | async-start | bytes 2621440 | tf_op jit(solution)/shard_map/all_gather | solution.py:242
  12.1 14.7 %collective-permute-start.1 = (bf16[128,1024]{0,1:T(8,128)(2,1)S(1)}, bf16[128,1024]{0,1:T(8,128)(2,1)S(1)}, u32[]{:S(2)}, u32[]{:S(2)}) collective-permute-start(bf16[128,1024]{0,1:T(8,128)(2,1)S(1)} %get-tuple-element.421), channel_id=1, source_target_pairs={{4,0},{8,4},{12,8},{0,12},{5,1},{9,5},{13,9},{1,13},{6,2},{10,6},{... | collective-permute-start | bytes 786440 | tf_op jit(solution)/shard_map/ppermute | solution.py:21
  17.2 19.7 %collective-permute-start = (bf16[128,1024]{0,1:T(8,128)(2,1)S(1)}, bf16[128,1024]{0,1:T(8,128)(2,1)S(1)}, u32[]{:S(2)}, u32[]{:S(2)}) collective-permute-start(bf16[128,1024]{0,1:T(8,128)(2,1)S(1)} %get-tuple-element.420), channel_id=1, source_target_pairs={{0,4},{4,8},{8,12},{12,0},{1,5},{5,9},{9,13},{13,1},{2,6},{6,10},{... | collective-permute-start | bytes 786440 | tf_op jit(solution)/shard_map/ppermute | solution.py:20
  38.1 10.1 %copy-start.1 = (bf16[512,512]{0,1:T(8,128)(2,1)S(1)}, bf16[512,512]{0,1:T(8,128)(2,1)}, u32[]{:S(2)}) copy-start(bf16[512,512]{0,1:T(8,128)(2,1)} %get-tuple-element.419) | copy-start | bytes 1572868
  38.2 133.0 %all-gather.11.cloned.1.call-start = ((), (), s32[]{:S(2)}) async-start(), calls=%async_computation.3 | async-start | bytes 2621440 | tf_op jit(solution)/shard_map/all_gather | solution.py:243
  79.4 6.0 %copy-start = (f32[4,512,1024]{2,1,0:T(8,128)S(1)}, f32[4,512,1024]{2,1,0:T(8,128)}, u32[]{:S(2)}) copy-start(f32[4,512,1024]{2,1,0:T(8,128)} %get-tuple-element.426) | copy-start | bytes 25165828
  85.3 7.1 %copy-start.3 = (bf16[512,512]{0,1:T(8,128)(2,1)S(1)}, bf16[512,512]{0,1:T(8,128)(2,1)}, u32[]{:S(2)}) copy-start(bf16[512,512]{0,1:T(8,128)(2,1)} %get-tuple-element.418) | copy-start | bytes 1572868
  85.3 7.1 %copy-start.4 = (bf16[1024,512]{0,1:T(8,128)(2,1)S(1)}, bf16[1024,512]{0,1:T(8,128)(2,1)}, u32[]{:S(2)}) copy-start(bf16[1024,512]{0,1:T(8,128)(2,1)} %all-gather.5.cloned.1.call-done) | copy-start | bytes 3145732
  172.8 4.0 %copy-start.6 = (f32[256,4,128]{0,2,1:T(8,128)S(1)}, f32[256,4,128]{0,2,1:T(8,128)}, u32[]{:S(2)}) copy-start(f32[256,4,128]{0,2,1:T(8,128)} %get-tuple-element.522) | copy-start | bytes 1572868 | tf_op jit(solution)/shard_map/while
  176.9 4.5 %copy-start.8 = (f32[256,4,128]{0,2,1:T(8,128)S(1)}, f32[256,4,128]{0,2,1:T(8,128)}, u32[]{:S(2)}) copy-start(f32[256,4,128]{0,2,1:T(8,128)} %get-tuple-element.523) | copy-start | bytes 1572868 | tf_op jit(solution)/shard_map/while
  181.4 3.3 %copy-start.7 = (f32[256,4,128]{0,2,1:T(8,128)}, f32[256,4,128]{0,2,1:T(8,128)S(1)}, u32[]{:S(2)}) copy-start(f32[256,4,128]{0,2,1:T(8,128)S(1)} %fusion.120) | copy-start | bytes 1572868 | tf_op jit(solution)/shard_map/while
  184.7 0.8 copy-start.9
  187.3 4.0 %copy-start.6 = (f32[256,4,128]{0,2,1:T(8,128)S(1)}, f32[256,4,128]{0,2,1:T(8,128)}, u32[]{:S(2)}) copy-start(f32[256,4,128]{0,2,1:T(8,128)} %get-tuple-element.522) | copy-start | bytes 1572868 | tf_op jit(solution)/shard_map/while
  191.3 4.5 %copy-start.8 = (f32[256,4,128]{0,2,1:T(8,128)S(1)}, f32[256,4,128]{0,2,1:T(8,128)}, u32[]{:S(2)}) copy-start(f32[256,4,128]{0,2,1:T(8,128)} %get-tuple-element.523) | copy-start | bytes 1572868 | tf_op jit(solution)/shard_map/while
  195.8 3.3 %copy-start.7 = (f32[256,4,128]{0,2,1:T(8,128)}, f32[256,4,128]{0,2,1:T(8,128)S(1)}, u32[]{:S(2)}) copy-start(f32[256,4,128]{0,2,1:T(8,128)S(1)} %fusion.120) | copy-start | bytes 1572868 | tf_op jit(solution)/shard_map/while
  199.1 0.8 copy-start.9
Sparse Core Ops, SparseCore 0:
  10.2 38.0 all-gather.4
  49.9 27.1 all-gather.6
  78.6 46.3 all-gather.8
  126.5 44.6 all-gather.10
where the time goes:
time: 211 us; the launch traced here: 210 us
  waiting for transfers between devices  93.5 us (44%)
  matrix products  43.7 us (21%)
  blocking collectives  26.7 us (13%)
  local copies, waits for them, and re-layouts  19.2 us (9%)
  between operations  14 us (7%)
  other arithmetic  7.86 us (4%)
  starting transfers between devices  5.26 us (2%)
    all_gather x1, waiting for transfers between devices, body(): lax.all_gather(cotan_slots.reshape(slot_rows, model_width), 'tm', axis=0,...  43.1 us
    all_gather x1, waiting for transfers between devices, body(): lax.all_gather(value_rows, 'tm', axis=0, tiled=True)  22.5 us
    all_gather x1, blocking collectives, body(): lax.all_gather(log_norm, 'tm', axis=0, tiled=True)  13.4 us
    all_gather x1, blocking collectives, body(): lax.all_gather(deltas, 'tm', axis=0, tiled=True)  13.3 us
    ppermute x1, waiting for transfers between devices, extended_2(): before = lax.ppermute(last, axis, up)  10.1 us
    ppermute x1, waiting for transfers between devices, extended_2(): after = lax.ppermute(first, axis, down)  9.6 us
    dot_general x2, matrix products, owner_work(): jnp.einsum('qhk,qhd->khd', score_grad, query_three, preferred_element_typ...  9.05 us
    unnamed x27, local copies, waits for them, and re-layouts  8.95 us
  transfers between devices with their start and end apart: 6, of which 5 were waited for; matrix products, arithmetic and copies ran while one was open for 17% of the time, Pallas kernels for 0%

commit v1 on v0

--- a/solution.py
+++ b/solution.py
@@ -8,6 +8,19 @@
 BLK = 128
 CAP = 1
 very_low = -1e30
+
+
+def ring_gather(array, axis, dim):
+    ways = lax.axis_size(axis)
+    up = [(d, (d + 1) % ways) for d in range(ways)]
+    down = [(d, (d - 1) % ways) for d in range(ways)]
+    earlier, later = ([array], [array])
+    for _ in range(ways // 2):
+        earlier.append(lax.ppermute(earlier[-1], axis, up))
+    for _ in range((ways - 1) // 2):
+        later.append(lax.ppermute(later[-1], axis, down))
+    line = jnp.concatenate([*earlier[::-1], *later[1:]], axis=dim)
+    return jnp.roll(line, (lax.axis_index(axis) - ways // 2) * array.shape[dim], axis=dim)
 
 
 def extended_2(shard, sides, width):
@@ -114,7 +127,7 @@
     )
     keys_all, values_all = (
         lax.all_gather(key_rows, "tm", axis=0, tiled=True),
-        lax.all_gather(value_rows, "tm", axis=0, tiled=True),
+        ring_gather(value_rows, "tm", 0),
     )
 
     def own_scores(key_piece, offset):

time: 211 us -> 188 us (0.89)
  waiting for transfers between devices: 93.5 us -> 73.9 us
  starting transfers between devices: 5.26 us -> 12.3 us
  other arithmetic: 7.86 us -> 3.55 us
  matrix products: 43.7 us -> 39.7 us
    all_gather x1 -> x0, waiting for transfers between devices: 22.5 us -> none  [body(): lax.all_gather(value_rows, 'tm', axis=0, tiled=True)]
    ppermute x0 -> x3, waiting for transfers between devices: none -> 17.6 us  [the longest x2 17.6 us: ring_gather(): earlier.append(lax.ppermute(earlier[-1], axis, up))]
    all_gather x1, waiting for transfers between devices: 7.42 us -> 0.01 us  [body(): lax.all_gather(key_rows, 'tm', axis=0, tiled=True)]
    ppermute x0 -> x3, starting transfers between devices: none -> 7.11 us  [the longest x2 5.75 us: ring_gather(): earlier.append(lax.ppermute(earlier[-1], axis, up))]
    all_gather x1, waiting for transfers between devices: 43.1 us -> 37.2 us  [body(): lax.all_gather(cotan_slots.reshape(slot_rows, model_width), 'tm', axis=0,...]
    dot_general x1, matrix products: 6.24 us -> 3.17 us  [own_scores(): jnp.einsum('qhd,khd->qhk', query_slots, key_piece, preferred_element_type...]
    all_gather x1 -> x0, local copies, waits for them, and re-layouts: 2.3 us -> none  [body(): lax.all_gather(value_rows, 'tm', axis=0, tiled=True)]
    reduce_sum x1, other arithmetic: 5.31 us -> 3.08 us  [forward(): masses = masses * shrink + jnp.sum(weights, axis=2)]
  transfers between devices with their start and end apart: 6 -> 8, of which waited for: 5 -> 5; matrix products, arithmetic and copies ran while one was open for 17% -> 16% of each run, Pallas kernels for 0% -> 0%
where the time goes in v1:
time: 188 us
  waiting for transfers between devices  73.9 us (39%)
  matrix products  39.7 us (21%)
  blocking collectives  26.7 us (14%)
  local copies, waits for them, and re-layouts  17.3 us (9%)
  between operations  14.1 us (8%)
  starting transfers between devices  12.3 us (7%)
  other arithmetic  3.55 us (2%)
    all_gather x1, waiting for transfers between devices, body(): lax.all_gather(cotan_slots.reshape(slot_rows, model_width), 'tm', axis=0,...  37.2 us
    ppermute x2, waiting for transfers between devices, ring_gather(): earlier.append(lax.ppermute(earlier[-1], axis, up))  17.6 us
    all_gather x1, blocking collectives, body(): lax.all_gather(log_norm, 'tm', axis=0, tiled=True)  13.4 us
    all_gather x1, blocking collectives, body(): lax.all_gather(deltas, 'tm', axis=0, tiled=True)  13.3 us
    ppermute x1, waiting for transfers between devices, extended_2(): before = lax.ppermute(last, axis, up)  10.1 us
    unnamed x40, local copies, waits for them, and re-layouts  9.61 us
    dot_general x2, matrix products, owner_work(): jnp.einsum('qhk,qhd->khd', score_grad, query_three, preferred_element_typ...  8.93 us
    dot_general x1, matrix products, query_pass(): jnp.einsum('qhk,khd->qhd', score_grad, key_piece, preferred_element_type=...  8.87 us
  transfers between devices with their start and end apart: 8, of which 5 were waited for; matrix products, arithmetic and copies ran while one was open for 16% of the time, Pallas kernels for 0%

profile of v1, /device:TPU:0, one launch (start us, length us, event | category | flops | bytes accessed | tf_op | source)
XLA Modules:
  0.0 187.6 jit_solution(10985440433408091893)
XLA Ops:
  7.2 0.0 copy-start.2
  7.2 0.0 copy-start.9
  7.2 0.0 copy-start.11
  7.2 0.0 copy-start.10
  7.2 0.0 all-gather.4.cloned.1.call-start
  7.3 1.8 copy.80
  9.1 0.0 all-gather.4.cloned.1.call-update
  9.1 0.0 all-gather.6.cloned.1.call-start
  9.2 1.1 copy.78
  10.2 1.1 copy.79
  11.4 5.1 %collective-permute-start.1 = (bf16[128,1024]{0,1:T(8,128)(2,1)S(1)}, bf16[128,1024]{0,1:T(8,128)(2,1)S(1)}, u32[]{:S(2)}, u32[]{:S(2)}) collective-permute-start(bf16[128,1024]{0,1:T(8,128)(2,1)S(1)} %get-tuple-element.421), channel_id=1, source_target_pairs={{4,0},{8,4},{12,8},{0,12},{5,1},{9,5},{13,9},{1,13},{6,2},{10,6},{... | collective-permute-start | bytes 786440 | tf_op jit(solution)/shard_map/ppermute | solution.py:34
  16.5 0.0 collective-permute-start
  16.5 8.8 %collective-permute-done.1 = bf16[128,1024]{0,1:T(8,128)(2,1)S(1)} collective-permute-done((bf16[128,1024]{0,1:T(8,128)(2,1)S(1)}, bf16[128,1024]{0,1:T(8,128)(2,1)S(1)}, u32[]{:S(2)}, u32[]{:S(2)}) %collective-permute-start.1) | collective-permute-done | bytes 262176 | tf_op jit(solution)/shard_map/ppermute | solution.py:34
  25.3 10.1 %collective-permute-done = bf16[128,1024]{0,1:T(8,128)(2,1)S(1)} collective-permute-done((bf16[128,1024]{0,1:T(8,128)(2,1)S(1)}, bf16[128,1024]{0,1:T(8,128)(2,1)S(1)}, u32[]{:S(2)}, u32[]{:S(2)}) %collective-permute-start) | collective-permute-done | bytes 262176 | tf_op jit(solution)/shard_map/ppermute | solution.py:33
  35.5 0.1 pad_maximum_fusion
  35.6 1.1 fusion.82
  36.7 0.0 all-gather.6.cloned.1.call-update
  36.7 0.0 all-gather.8.cloned.1.call-start
  36.7 0.0 copy-done.2
  36.7 2.5 %collective-permute-start.2 = (bf16[256,512]{1,0:T(8,128)(2,1)S(1)}, bf16[256,512]{1,0:T(8,128)(2,1)S(1)}, u32[]{:S(2)}, u32[]{:S(2)}) collective-permute-start(bf16[256,512]{1,0:T(8,128)(2,1)S(1)} %copy-done.2), channel_id=1, source_target_pairs={{0,4},{4,8},{8,12},{12,0},{1,5},{5,9},{9,13},{13,1},{2,6},{6,10},{... | collective-permute-start | bytes 786440 | tf_op jit(solution)/shard_map/ppermute | solution.py:19
  39.3 1.4 collective-permute-start.4
  40.6 0.0 copy-done.9
  40.7 0.1 select_reduce_fusion.3
  40.8 0.2 fusion.63
  40.9 0.2 convolution_multiply_fusion
  41.2 0.1 dynamic-slice_compare_fusion
  41.3 0.1 broadcast_bitcast_fusion
  41.3 12.0 %collective-permute-done.2 = bf16[256,512]{1,0:T(8,128)(2,1)S(1)} collective-permute-done((bf16[256,512]{1,0:T(8,128)(2,1)S(1)}, bf16[256,512]{1,0:T(8,128)(2,1)S(1)}, u32[]{:S(2)}, u32[]{:S(2)}) %collective-permute-start.2) | collective-permute-done | bytes 262176 | tf_op jit(solution)/shard_map/ppermute | solution.py:19
  53.3 3.2 %collective-permute-start.3 = (bf16[256,512]{1,0:T(8,128)(2,1)S(1)}, bf16[256,512]{1,0:T(8,128)(2,1)S(1)}, u32[]{:S(2)}, u32[]{:S(2)}) collective-permute-start(bf16[256,512]{1,0:T(8,128)(2,1)S(1)} %collective-permute-done.2), channel_id=1, source_target_pairs={{0,4},{4,8},{8,12},{12,0},{1,5},{5,9},{9,13},{13,1},{2,6},{6,10},{... | collective-permute-start | bytes 786440 | tf_op jit(solution)/shard_map/ppermute | solution.py:19
  56.6 0.1 copy.89
  56.7 0.1 copy.88
  56.9 0.2 copy.90
  57.1 0.8 copy.91
  57.9 0.6 convolution_compare_fusion.1
  58.5 0.0 all-gather.8.cloned.1.call-update
  58.5 5.6 %collective-permute-done.3 = bf16[256,512]{1,0:T(8,128)(2,1)S(1)} collective-permute-done((bf16[256,512]{1,0:T(8,128)(2,1)S(1)}, bf16[256,512]{1,0:T(8,128)(2,1)S(1)}, u32[]{:S(2)}, u32[]{:S(2)}) %collective-permute-start.3) | collective-permute-done | bytes 262176 | tf_op jit(solution)/shard_map/ppermute | solution.py:19
  64.2 0.0 collective-permute-done.4
  64.3 0.1 constant_dynamic-slice_fusion.4
  64.4 1.3 copy.83
  65.8 3.2 %fusion.34 = (f32[512,4]{0,1:T(4,128)S(1)}, f32[4,512,1024]{2,1,0:T(8,128)S(1)}) fusion(pred[512,1024]{1,0:T(8,128)(4,1)S(1)} %convolution_compare_fusion.1, bf16[512,4,128]{0,2,1:T(8,128)(2,1)S(1)} %bitcast.173, bf16[1024,4,128]{0,2,1:T(8,128)(2,1)} %bitcast.176), kind=kOutput, calls=%fused_computation.46 | convolution fusion | flops 543160320 | bytes 10493952 | tf_op jit(solution)/shard_map/qhd,khd->qhk/dot_general | solution.py:144
  69.0 3.1 %fusion.41 = f32[512,4]{0,1:T(4,128)S(1)} fusion(f32[4,512,1024]{2,1,0:T(8,128)S(1)} %get-tuple-element.426, f32[512,4]{0,1:T(4,128)S(1)} %broadcast_maximum_fusion, pred[512,1024]{1,0:T(8,128)(4,1)S(1)} %convolution_compare_fusion.1), kind=kLoop, calls=%fused_computation.53 | loop fusion | flops 10483712 | bytes 8929280 | tf_op jit(solution)/shard_map/reduce_sum | solution.py:159
  72.1 0.1 copy-done
  72.2 0.0 copy-done.6
  72.2 3.6 %multiply_reduce_fusion = (f32[512,4]{0,1:T(4,128)S(1)}, bf16[512,4,128]{0,2,1:T(8,128)(2,1)}) fusion(bf16[512,1024]{0,1:T(8,128)(2,1)S(1)} %pad_maximum_fusion, f32[512,4]{0,1:T(4,128)S(1)} %get-tuple-element.413, bf16[1024,4,128]{0,2,1:T(8,128)(2,1)S(1)} %bitcast.181, f32[4,512,1024]{2,1,0:T(8,128)S(1)} %get-tuple-element.426, ...), kind=kOutput, calls=%fused_computation.69 | convolution fusion | flops 549189632 | bytes 11042816 | tf_op jit(solution)/shard_map/qhk,khd->qhd/dot_general | solution.py:160
  75.8 2.1 %copy.94 = bf16[512,512]{1,0:T(8,128)(2,1)} copy(bf16[512,512]{0,1:T(8,128)(2,1)} %bitcast.183) | data formatting | bytes 1048576
  77.9 0.0 copy-done.5
  77.9 8.9 %fusion.60 = bf16[4,512,128]{1,2,0:T(8,128)(2,1)} fusion(bf16[1024,4,128]{0,2,1:T(8,128)(2,1)S(1)} %bitcast.177, f32[4,512,1024]{2,1,0:T(8,128)} %copy-done, f32[512,4]{0,1:T(4,128)S(1)} %get-tuple-element.427, f32[512,4]{0,1:T(4,128)S(1)} %get-tuple-element.412, pred[512,1024]{1,0:T(8,128)(4,1)S(1)} %convolution_compare_fusion.1, ...), kind=kOutput, calls=%fused_computation.64 | convolution fusion | flops 1088946176 | bytes 12075008 | tf_op jit(solution)/shard_map/qhk,khd->qhd/dot_general | solution.py:195
  86.7 2.1 %copy.95 = bf16[512,512]{1,0:T(8,128)(2,1)} copy(bf16[512,512]{0,1:T(8,128)(2,1)} %bitcast.184) | data formatting | bytes 1048576
  88.8 13.4 %all_gather.17 = f32[2048,4]{0,1:T(4,128)S(1)} all-gather(f32[512,4]{0,1:T(4,128)S(1)} %get-tuple-element.412), channel_id=1, replica_groups=mesh['groups'=2,'tm'=4,'head'=2,'mp'=2] {'tm'}, dimensions={0}, use_global_device_ids=true | all-gather | bytes 40960 | tf_op jit(solution)/shard_map/all_gather | solution.py:205
  102.2 13.3 %all_gather.19 = f32[2048,4]{0,1:T(4,128)S(1)} all-gather(f32[512,4]{0,1:T(4,128)S(1)} %get-tuple-element.427), channel_id=1, replica_groups=mesh['groups'=2,'tm'=4,'head'=2,'mp'=2] {'tm'}, dimensions={0}, use_global_device_ids=true | all-gather | bytes 40960 | tf_op jit(solution)/shard_map/all_gather | solution.py:206
  115.5 37.2 %all-gather.8.cloned.1.call-done = bf16[2048,512]{0,1:T(8,128)(2,1)} async-done(((bf16[512,512]{0,1:T(8,128)(2,1)}), bf16[2048,512]{0,1:T(8,128)(2,1)}) %all-gather.8.cloned.1.call-update) | async-done | bytes 2097168 | tf_op jit(solution)/shard_map/all_gather | solution.py:256
  152.7 26.6 %while.18 = (s32[]{:T(128)}, f32[256,4,128]{0,2,1:T(8,128)S(1)}, f32[256,4,128]{0,2,1:T(8,128)S(1)}, bf16[2048,512]{0,1:T(8,128)(2,1)}, bf16[16,8]{0,1:T(8,128)(...) while((s32[]{:T(128)}, f32[256,4,128]{0,2,1:T(8,128)S(1)}, ...), condition=%wide.region_8.9_spmd.clone, body=%wide.region_7.8_spmd.clone.sunk | while | flops 1091612672 | bytes 24503768 | solution.py:101
  152.7 1.7 constant_dynamic-slice_fusion.7
  154.4 2.7 %fusion.119 = f32[4,1024,256]{2,1,0:T(8,128)} fusion(bf16[1024,4,128]{0,2,1:T(8,128)(2,1)S(1)} %bitcast.169, bf16[256,4,128]{2,0,1:T(8,128)(2,1)S(1)} %get-tuple-element.543), kind=kOutput, calls=%fused_computation.143.clone.1 | convolution fusion | flops 268435456 | bytes 5505024 | tf_op jit(solution)/shard_map/while/body/eval_jaxpr/qhd,khd->qhk/dot_general | solution.py:229
  157.1 1.3 convolution_compare_fusion.3
  158.4 4.5 %fusion.120 = f32[256,4,128]{0,2,1:T(8,128)S(1)} fusion(bf16[1024,4,128]{0,2,1:T(8,128)(2,1)S(1)} %bitcast.170, f32[4,1024,256]{2,1,0:T(8,128)} %fusion.119, bf16[1024,4,128]{0,2,1:T(8,128)(2,1)S(1)} %bitcast.171, bf16[256,4,128]{2,0,1:T(8,128)(2,1)} %get-tuple-element.546, f32[1024,4]{0,1:T(4,128)S(1)} %get-tuple-element.506, ...), kind=kOutput, calls=%fused_computation.16.clone.1 | convolution fusion | flops 544473088 | bytes 7897089 | tf_op jit(solution)/shard_map/while/body/eval_jaxpr/qhk,qhd->khd/dot_general | solution.py:239
  162.9 3.1 %fusion.121 = f32[256,4,128]{0,2,1:T(8,128)S(1)} fusion(bf16[1024,4,128]{0,2,1:T(8,128)(2,1)S(1)} %bitcast.172, f32[4,1024,256]{2,1,0:T(8,128)} %fusion.119, f32[1024,4]{0,1:T(4,128)S(1)} %get-tuple-element.507, pred[1024,256]{1,0:T(8,128)(4,1)} %convolution_compare_fusion.3, f32[256,4,128]{0,2,1:T(8,128)S(1)} %get-tuple-element.525, pred[]{:T(512)S(6)} %compare.54), kind=kOutput, calls=%fused_computation.15.clone.1 | convolution fusion | flops 273940480 | bytes 6569985 | tf_op jit(solution)/shard_map/while/body/eval_jaxpr/qhk,qhd->khd/dot_general | solution.py:242
  166.0 1.7 constant_dynamic-slice_fusion.7
  167.7 2.7 %fusion.119 = f32[4,1024,256]{2,1,0:T(8,128)} fusion(bf16[1024,4,128]{0,2,1:T(8,128)(2,1)S(1)} %bitcast.169, bf16[256,4,128]{2,0,1:T(8,128)(2,1)S(1)} %get-tuple-element.543), kind=kOutput, calls=%fused_computation.143.clone.1 | convolution fusion | flops 268435456 | bytes 5505024 | tf_op jit(solution)/shard_map/while/body/eval_jaxpr/qhd,khd->qhk/dot_general | solution.py:229
  170.5 1.3 convolution_compare_fusion.3
  171.8 4.5 %fusion.120 = f32[256,4,128]{0,2,1:T(8,128)S(1)} fusion(bf16[1024,4,128]{0,2,1:T(8,128)(2,1)S(1)} %bitcast.170, f32[4,1024,256]{2,1,0:T(8,128)} %fusion.119, bf16[1024,4,128]{0,2,1:T(8,128)(2,1)S(1)} %bitcast.171, bf16[256,4,128]{2,0,1:T(8,128)(2,1)} %get-tuple-element.546, f32[1024,4]{0,1:T(4,128)S(1)} %get-tuple-element.506, ...), kind=kOutput, calls=%fused_computation.16.clone.1 | convolution fusion | flops 544473088 | bytes 7897089 | tf_op jit(solution)/shard_map/while/body/eval_jaxpr/qhk,qhd->khd/dot_general | solution.py:239
  176.3 3.1 %fusion.121 = f32[256,4,128]{0,2,1:T(8,128)S(1)} fusion(bf16[1024,4,128]{0,2,1:T(8,128)(2,1)S(1)} %bitcast.172, f32[4,1024,256]{2,1,0:T(8,128)} %fusion.119, f32[1024,4]{0,1:T(4,128)S(1)} %get-tuple-element.507, pred[1024,256]{1,0:T(8,128)(4,1)} %convolution_compare_fusion.3, f32[256,4,128]{0,2,1:T(8,128)S(1)} %get-tuple-element.525, pred[]{:T(512)S(6)} %compare.54), kind=kOutput, calls=%fused_computation.15.clone.1 | convolution fusion | flops 273940480 | bytes 6569985 | tf_op jit(solution)/shard_map/while/body/eval_jaxpr/qhk,qhd->khd/dot_general | solution.py:242
  179.4 0.8 copy.104
  180.3 0.8 copy.105
  (43 shorter events, 0.4 us)
Async XLA Ops:
  7.2 29.6 %copy-start.2 = (bf16[256,512]{1,0:T(8,128)(2,1)S(1)}, bf16[256,512]{1,0:T(8,128)(2,1)}, u32[]{:S(2)}) copy-start(bf16[256,512]{1,0:T(8,128)(2,1)} %param.11) | copy-start | bytes 786436
  7.2 33.5 %copy-start.9 = (s32[4,2]{0,1:T(2,128)S(1)}, s32[4,2]{0,1:T(2,128)}, u32[]{:S(2)}) copy-start(s32[4,2]{0,1:T(2,128)} %param.14) | copy-start | bytes 100
  7.2 33.6 %copy-start.11 = (s32[8]{0:T(128)S(1)}, s32[8]{0:T(128)}, u32[]{:S(2)}) copy-start(s32[8]{0:T(128)} %param.13) | copy-start | bytes 100
  7.2 33.7 %copy-start.10 = (s32[8,8]{1,0:T(8,128)S(1)}, s32[8,8]{1,0:T(8,128)}, u32[]{:S(2)}) copy-start(s32[8,8]{1,0:T(8,128)} %param.15) | copy-start | bytes 772
  7.2 58.5 %all-gather.4.cloned.1.call-start = ((), (), s32[]{:S(2)}) async-start(), calls=%async_computation | async-start | bytes 1310720 | tf_op jit(solution)/shard_map/all_gather | solution.py:129
  9.1 47.8 %copy-start.3 = (bf16[256,512]{0,1:T(8,128)(2,1)S(1)}, bf16[256,512]{0,1:T(8,128)(2,1)}, u32[]{:S(2)}) copy-start(bf16[256,512]{0,1:T(8,128)(2,1)} %copy.80) | copy-start | bytes 786436
  9.1 106.3 %all-gather.6.cloned.1.call-start = ((), (), s32[]{:S(2)}) async-start(), calls=%async_computation.1 | async-start | bytes 2621440 | tf_op jit(solution)/shard_map/all_gather | solution.py:255
  11.4 14.0 %collective-permute-start.1 = (bf16[128,1024]{0,1:T(8,128)(2,1)S(1)}, bf16[128,1024]{0,1:T(8,128)(2,1)S(1)}, u32[]{:S(2)}, u32[]{:S(2)}) collective-permute-start(bf16[128,1024]{0,1:T(8,128)(2,1)S(1)} %get-tuple-element.421), channel_id=1, source_target_pairs={{4,0},{8,4},{12,8},{0,12},{5,1},{9,5},{13,9},{1,13},{6,2},{10,6},{... | collective-permute-start | bytes 786440 | tf_op jit(solution)/shard_map/ppermute | solution.py:34
  16.5 19.0 %collective-permute-start = (bf16[128,1024]{0,1:T(8,128)(2,1)S(1)}, bf16[128,1024]{0,1:T(8,128)(2,1)S(1)}, u32[]{:S(2)}, u32[]{:S(2)}) collective-permute-start(bf16[128,1024]{0,1:T(8,128)(2,1)S(1)} %get-tuple-element.420), channel_id=1, source_target_pairs={{0,4},{4,8},{8,12},{12,0},{1,5},{5,9},{9,13},{13,1},{2,6},{6,10},{... | collective-permute-start | bytes 786440 | tf_op jit(solution)/shard_map/ppermute | solution.py:33
  36.7 116.0 %all-gather.8.cloned.1.call-start = ((), (), s32[]{:S(2)}) async-start(), calls=%async_computation.2 | async-start | bytes 2621440 | tf_op jit(solution)/shard_map/all_gather | solution.py:256
  36.7 16.6 %collective-permute-start.2 = (bf16[256,512]{1,0:T(8,128)(2,1)S(1)}, bf16[256,512]{1,0:T(8,128)(2,1)S(1)}, u32[]{:S(2)}, u32[]{:S(2)}) collective-permute-start(bf16[256,512]{1,0:T(8,128)(2,1)S(1)} %copy-done.2), channel_id=1, source_target_pairs={{0,4},{4,8},{8,12},{12,0},{1,5},{5,9},{9,13},{13,1},{2,6},{6,10},{... | collective-permute-start | bytes 786440 | tf_op jit(solution)/shard_map/ppermute | solution.py:19
  39.3 24.9 %collective-permute-start.4 = (bf16[256,512]{1,0:T(8,128)(2,1)S(1)}, bf16[256,512]{1,0:T(8,128)(2,1)S(1)}, u32[]{:S(2)}, u32[]{:S(2)}) collective-permute-start(bf16[256,512]{1,0:T(8,128)(2,1)S(1)} %copy-done.2), channel_id=1, source_target_pairs={{0,12},{4,0},{8,4},{12,8},{1,13},{5,1},{9,5},{13,9},{2,14},{6,2},{... | collective-permute-start | bytes 786440 | tf_op jit(solution)/shard_map/ppermute | solution.py:21
  53.3 10.8 %collective-permute-start.3 = (bf16[256,512]{1,0:T(8,128)(2,1)S(1)}, bf16[256,512]{1,0:T(8,128)(2,1)S(1)}, u32[]{:S(2)}, u32[]{:S(2)}) collective-permute-start(bf16[256,512]{1,0:T(8,128)(2,1)S(1)} %collective-permute-done.2), channel_id=1, source_target_pairs={{0,4},{4,8},{8,12},{12,0},{1,5},{5,9},{9,13},{13,1},{2,6},{6,10},{... | collective-permute-start | bytes 786440 | tf_op jit(solution)/shard_map/ppermute | solution.py:19
  58.5 7.2 %copy-start.1 = (bf16[512,512]{0,1:T(8,128)(2,1)S(1)}, bf16[512,512]{0,1:T(8,128)(2,1)}, u32[]{:S(2)}) copy-start(bf16[512,512]{0,1:T(8,128)(2,1)} %get-tuple-element.419) | copy-start | bytes 1572868
  68.9 3.2 %copy-start = (f32[4,512,1024]{2,1,0:T(8,128)}, f32[4,512,1024]{2,1,0:T(8,128)S(1)}, u32[]{:S(2)}) copy-start(f32[4,512,1024]{2,1,0:T(8,128)S(1)} %get-tuple-element.426) | copy-start | bytes 25165828
  68.9 3.2 %copy-start.6 = (bf16[1024,512]{0,1:T(8,128)(2,1)S(1)}, bf16[1024,512]{0,1:T(8,128)(2,1)}, u32[]{:S(2)}) copy-start(bf16[1024,512]{0,1:T(8,128)(2,1)} %copy.83) | copy-start | bytes 3145732
  72.2 5.7 %copy-start.4 = (bf16[512,512]{0,1:T(8,128)(2,1)S(1)}, bf16[512,512]{0,1:T(8,128)(2,1)}, u32[]{:S(2)}) copy-start(bf16[512,512]{0,1:T(8,128)(2,1)} %get-tuple-element.418) | copy-start | bytes 1572868
  72.2 5.7 %copy-start.5 = (bf16[1024,512]{0,1:T(8,128)(2,1)S(1)}, bf16[1024,512]{0,1:T(8,128)(2,1)}, u32[]{:S(2)}) copy-start(bf16[1024,512]{0,1:T(8,128)(2,1)} %all-gather.4.cloned.1.call-done) | copy-start | bytes 3145732
  77.9 74.8 %copy-start.7 = (f32[256,4,128]{0,2,1:T(8,128)S(1)}, f32[256,4,128]{0,2,1:T(8,128)}, u32[]{:S(2)}) copy-start(f32[256,4,128]{0,2,1:T(8,128)} %custom-call) | copy-start | bytes 1572868
  77.9 74.8 %copy-start.8 = (f32[256,4,128]{0,2,1:T(8,128)S(1)}, f32[256,4,128]{0,2,1:T(8,128)}, u32[]{:S(2)}) copy-start(f32[256,4,128]{0,2,1:T(8,128)} %custom-call.1) | copy-start | bytes 1572868
Sparse Core Ops, SparseCore 0:
  10.2 48.4 all-gather.3
  60.2 46.1 all-gather.5
  108.0 44.6 all-gather.7
